TPU v7x, 32 devices: a whole 2x2x4 slice. The times are simulated.
32 devices in a mesh: groups: 2 (over x), mem: 16 (over z, y, core).
Axes of the slice: x: 2, y: 2, z: 4, core: 2. Of those that a mesh axis runs over, the one named last changes fastest.
Arguments:
- mem_key: bfloat16 [128, 128, 128], P(('groups', 'mem')), parts along dimension 0, may hold values from -6 to 6
- value_base: bfloat16 [128, 128, 512], P(('groups', 'mem')), parts along dimension 0, may hold values from -6 to 6
- memory_labels: int32 [128, 128], P(('groups', 'mem')), parts along dimension 0, may hold values from 0 to 7
- valid_counts: int32 [32], P(('groups', 'mem')), parts along dimension 0, may hold values from 128 to 512, as said below
- query_key: bfloat16 [32, 64, 128], P(('groups', 'mem')), parts along dimension 0, may hold values from -96 to 96
- query_value: bfloat16 [32, 64, 512], P(('groups', 'mem')), parts along dimension 0, may hold values from -6 to 6
- object_embed: bfloat16 [8, 512], replicated, may hold values from -6 to 6
- decode_weight: bfloat16 [3, 3, 1024, 256], replicated, may hold values from -0.0625 to 0.0625
- mask_weight: bfloat16 [256, 8], replicated, may hold values from -0.375 to 0.375
Outputs:
- mask_logits: float32 [32, 64, 8], P(('groups', 'mem')), parts along dimension 0
There are 2 independent parts, one for each index of `groups`. A program takes and returns all parts, laid end to end along the dimension named above; an argument that names none is the same for every part. Nothing has to cross between parts.
Inputs may be any that keep to these rules, and one draw needn't show every extreme that they name: `valid_counts`: live positions of each memory block; some block is full and some holds a quarter.
All inputs are finite; a program needn't handle non-finite values.
Results may differ from a plain program's by a relative error of at most 0.0048.
Values may be sent and summed in bfloat16 or wider, within the bound.
A program may use at most 320 MiB of HBM per device.

v0:
```python
import math

import jax
import jax.numpy as jnp
from jax import lax
from jax.sharding import PartitionSpec as P


def with_halo(block, sides, width):
    for axis, dim in sides:
        count = lax.axis_size(axis)
        forward = [(i, i + 1) for i in range(count - 1)]
        backward = [(target, source) for source, target in forward]
        low = lax.ppermute(
            lax.slice_in_dim(block, block.shape[dim] - width, None, axis=dim), axis, forward
        )
        high = lax.ppermute(lax.slice_in_dim(block, 0, width, axis=dim), axis, backward)
        block = jnp.concatenate([low, block, high], axis=dim)
    return block


def conv_taps(padded, weight, height, width):
    summed = jnp.zeros((height * width, weight.shape[3]), jnp.float32)
    for row_step in range(3):
        for col_step in range(3):
            window = padded[row_step : row_step + height, col_step : col_step + width].reshape(
                height * width, -1
            )
            summed = summed + jnp.dot(
                window, weight[row_step, col_step], preferred_element_type=jnp.float32
            )
    return summed


def shards(
    mem_key,
    value_base,
    memory_labels,
    valid_counts,
    query_key,
    query_value,
    object_embed,
    decode_weight,
    mask_weight,
):
    key_width = mem_key.shape[2]
    val_width = value_base.shape[2]
    keys_local = mem_key.reshape(-1, key_width)
    onehot = (
        memory_labels.reshape(-1)[:, None]
        == jnp.arange(object_embed.shape[0], dtype=jnp.int32)[None, :]
    ).astype(jnp.bfloat16)
    embedded = jnp.dot(onehot, object_embed, preferred_element_type=jnp.float32)
    mem_value = (value_base.reshape(-1, val_width).astype(jnp.float32) + embedded).astype(
        jnp.bfloat16
    )
    queries = lax.all_gather(query_key, "mem", axis=0, tiled=True).reshape(-1, key_width)
    block_size = keys_local.shape[0]
    scores = jnp.dot(queries, keys_local.T, preferred_element_type=jnp.float32) * (
        1.0 / math.sqrt(key_width)
    )
    is_live = (jnp.arange(block_size, dtype=jnp.int32) < valid_counts[0])[None, :]
    scores = jnp.where(is_live, scores, -jnp.inf)
    block_peak = jnp.max(scores, axis=1)
    weights = jnp.where(is_live, jnp.exp(scores - block_peak[:, None]), 0.0).astype(jnp.bfloat16)
    block_mass = jnp.sum(weights.astype(jnp.float32), axis=1)
    block_values = jnp.dot(weights, mem_value, preferred_element_type=jnp.float32)
    query_height = query_value.shape[0]
    query_width = query_value.shape[1]
    owned = query_height * query_width
    largest = lax.pmax(block_peak, "mem")
    rescale = jnp.exp(block_peak - largest)
    scaled_mass = (rescale * block_mass).reshape(-1, query_width)
    scaled_values = (rescale[:, None] * block_values).reshape(-1, query_width, val_width)
    weight_sum, value_sums = (
        lax.psum_scatter(scaled_mass, "mem", scatter_dimension=0, tiled=True),
        lax.psum_scatter(scaled_values, "mem", scatter_dimension=0, tiled=True),
    )
    weight_sum = weight_sum.reshape(owned)
    value_sums = value_sums.reshape(owned, val_width)
    readout = (
        (value_sums / weight_sum[:, None])
        .astype(jnp.bfloat16)
        .reshape(query_height, query_width, val_width)
    )
    joined = jnp.concatenate([readout, query_value], axis=-1)
    bordered = with_halo(joined, (("mem", 0),), 1)
    bordered = jnp.pad(bordered, ((0, 0), (1, 1), (0, 0)))
    hidden = jax.nn.relu(conv_taps(bordered, decode_weight, query_height, query_width)).astype(
        jnp.bfloat16
    )
    logits = jnp.dot(hidden, mask_weight, preferred_element_type=jnp.float32)
    return logits.reshape(query_height, query_width, mask_weight.shape[1])


def solution(mesh):
    placed = (
        P(("groups", "mem"), None, None),
        P(("groups", "mem"), None, None),
        P(("groups", "mem"), None),
        P(("groups", "mem")),
        P(("groups", "mem"), None, None),
        P(("groups", "mem"), None, None),
        P(),
        P(),
        P(),
    )
    return jax.shard_map(
        shards,
        mesh=mesh,
        in_specs=placed,
        out_specs=P(("groups", "mem"), None, None),
        check_vma=False,
    )
```

profile of v0, /device:TPU:1, one launch (start us, length us, event | category | flops | bytes accessed | tf_op | source)
XLA Modules:
  0.0 153.7 jit_solution(16942197713252962668)
XLA Ops:
  6.5 0.0 copy-start
  6.5 0.0 reduce-scatter.2.cloned.1.call-start
  7.2 23.9 %all_gather.3 = bf16[16,64,128]{2,1,0:T(8,128)(2,1)S(1)} all-gather(bf16[1,64,128]{2,1,0:T(8,128)(2,1)} %param.13), channel_id=1, replica_groups=mesh['groups'=2,'mem'=16] {'mem'}, dimensions={0}, use_global_device_ids=true | all-gather | bytes 278528 | tf_op jit(solution)/shard_map/all_gather | solution.py:57
  31.2 0.0 copy-done
  31.2 0.5 fusion
  31.6 0.0 copy-start.3
  31.7 0.0 copy-start.4
  31.7 29.0 %pmax.7 = f32[1024]{0:T(1024)S(1)} all-reduce(f32[1024]{0:T(1024)S(1)} %get-tuple-element.9), channel_id=1, replica_groups=mesh['groups'=2,'mem'=16] {'mem'}, use_global_device_ids=true, to_apply=%region_1.2 | all-reduce | flops 1024 | bytes 8192 | tf_op jit(solution)/shard_map/pmax | solution.py:71
  60.7 0.6 convert_reduce_fusion
  61.3 0.0 copy-done.3
  61.3 0.0 copy-done.4
  61.3 0.0 copy-start.5
  61.3 3.4 %convolution_multiply_fusion = f32[1024,512]{1,0:T(8,128)} fusion(bf16[1024,512]{0,1:T(8,128)(2,1)S(1)} %get-tuple-element.8, bf16[8,512]{1,0:T(8,128)(2,1)S(1)} %copy-done.3, bf16[512,512]{1,0:T(8,128)(2,1)} %bitcast.77, f32[1024]{0:T(1024)S(1)} %get-tuple-element.6, s32[512]{0:T(512)S(1)} %bitcast.78), kind=kOutput, calls=%fused_computation.4 | convolution fusion | flops 542380032 | bytes 3684352 | tf_op jit(solution)/shard_map/dot_general | solution.py:67
  64.7 0.0 copy-start.1
  64.7 0.0 reduce-scatter.2.cloned.1.call-update
  64.7 0.1 reshape.64
  64.8 0.0 copy-done.5
  64.8 0.6 dynamic-slice
  65.4 30.5 %all-reduce.1 = f32[16,64]{1,0:T(8,128)S(1)} all-reduce(f32[16,64]{1,0:T(8,128)S(1)} %reshape.64), channel_id=3, replica_groups=mesh['groups'=2,'mem'=16] {'mem'}, use_global_device_ids=true, to_apply=%region_4.5.clone | all-reduce | flops 1024 | bytes 8192
  95.9 0.7 dynamic-slice_bitcast_fusion
  96.6 25.9 %reduce-scatter.2.cloned.1.call-done = f32[1,64,512]{2,1,0:T(8,128)} async-done(((f32[16,64,512]{2,1,0:T(8,128)}), f32[1,64,512]{2,1,0:T(8,128)}) %reduce-scatter.2.cloned.1.call-update) | async-done | bytes 131088 | tf_op jit(solution)/shard_map/reduce_scatter | solution.py:77
  122.5 1.0 divide_convert_fusion
  123.5 0.0 copy-done.1
  123.5 4.9 %collective-permute-start = (bf16[1,64,1024]{2,1,0:T(8,128)(2,1)S(1)}, bf16[1,64,1024]{2,1,0:T(8,128)(2,1)S(1)}, u32[]{:S(2)}, u32[]{:S(2)}) collective-permute-start(bf16[1,64,1024]{2,1,0:T(8,128)(2,1)S(1)} %pad_maximum_fusion), channel_id=1, source_target_pairs={{0,1},{1,2},{2,3},{3,4},{4,5},{5,6},{6,7},{7,8},{8,9},{9,10},{10,1... | collective-permute-start | bytes 393224 | tf_op jit(solution)/shard_map/ppermute | solution.py:14
  128.4 1.9 %collective-permute-start.1 = (bf16[1,64,1024]{2,1,0:T(8,128)(2,1)S(1)}, bf16[1,64,1024]{2,1,0:T(8,128)(2,1)S(1)}, u32[]{:S(2)}, u32[]{:S(2)}) collective-permute-start(bf16[1,64,1024]{2,1,0:T(8,128)(2,1)S(1)} %pad_maximum_fusion), channel_id=1, source_target_pairs={{1,0},{2,1},{3,2},{4,3},{5,4},{6,5},{7,6},{8,7},{9,8},{10,9},{11,1... | collective-permute-start | bytes 393224 | tf_op jit(solution)/shard_map/ppermute | solution.py:17
  130.3 0.0 collective-permute-done
  130.3 4.3 %collective-permute-done.1 = bf16[1,64,1024]{2,1,0:T(8,128)(2,1)S(1)} collective-permute-done((bf16[1,64,1024]{2,1,0:T(8,128)(2,1)S(1)}, bf16[1,64,1024]{2,1,0:T(8,128)(2,1)S(1)}, u32[]{:S(2)}, u32[]{:S(2)}) %collective-permute-start.1) | collective-permute-done | bytes 131104 | tf_op jit(solution)/shard_map/ppermute | solution.py:17
  134.7 0.1 select_maximum_fusion
  134.8 1.2 fusion.19
  136.0 1.2 fusion.9
  137.3 1.3 convolution_add_fusion.7
  138.6 0.0 copy-start.2
  138.6 1.3 convolution_add_fusion.6
  139.8 1.3 convolution_add_fusion.5
  141.1 1.3 convolution_add_fusion.4
  142.4 1.3 convolution_add_fusion.3
  143.6 1.3 convolution_add_fusion.2
  144.9 0.0 copy-done.2
  144.9 2.0 %fusion.6 = f32[1,64,8]{1,2,0:T(8,128)} fusion(bf16[256,8]{0,1:T(8,128)(2,1)S(1)} %copy-done.2, f32[64,256]{1,0:T(8,128)S(1)} %fusion.9, f32[64,256]{1,0:T(8,128)S(1)} %convolution_add_fusion.2, bf16[3,3,1024,256]{3,2,1,0:T(8,128)(2,1)} %param.16, bf16[1,64,1024]{2,1,0:T(8,128)(2,1)S(1)} %collective-permute-done.1), kind=kOutput, calls=%fused_computation.20 | convolution fusion | flops 33882112 | bytes 792576 | tf_op jit(solution)/shard_map/dot_general | solution.py:92
  (3 shorter events, 0.0 us)
Async XLA Ops:
  6.5 24.7 %copy-start = (bf16[4,128,128]{2,1,0:T(8,128)(2,1)S(1)}, bf16[4,128,128]{2,1,0:T(8,128)(2,1)}, u32[]{:S(2)}) copy-start(bf16[4,128,128]{2,1,0:T(8,128)(2,1)} %param.9) | copy-start | bytes 393220
  6.5 115.9 %reduce-scatter.2.cloned.1.call-start = ((), (), s32[]{:S(2)}) async-start(), calls=%async_computation.1 | async-start | bytes 2228224 | tf_op jit(solution)/shard_map/reduce_scatter | solution.py:77
  31.6 29.7 %copy-start.3 = (bf16[8,512]{1,0:T(8,128)(2,1)S(1)}, bf16[8,512]{1,0:T(8,128)(2,1)}, u32[]{:S(2)}) copy-start(bf16[8,512]{1,0:T(8,128)(2,1)} %param.15) | copy-start | bytes 24580
  31.7 29.6 %copy-start.4 = (s32[4,128]{1,0:T(4,128)S(1)}, s32[4,128]{1,0:T(4,128)}, u32[]{:S(2)}) copy-start(s32[4,128]{1,0:T(4,128)} %param.11) | copy-start | bytes 6148
  61.3 3.5 %copy-start.5 = (u32[32]{0:T(128)S(1)}, u32[32]{0:T(128)}, u32[]{:S(2)}) copy-start(u32[32]{0:T(128)} %constant.21) | copy-start | bytes 388
  64.7 58.8 %copy-start.1 = (bf16[1,64,512]{2,1,0:T(8,128)(2,1)S(1)}, bf16[1,64,512]{2,1,0:T(8,128)(2,1)}, u32[]{:S(2)}) copy-start(bf16[1,64,512]{2,1,0:T(8,128)(2,1)} %param.14) | copy-start | bytes 196612
  123.5 6.8 %collective-permute-start = (bf16[1,64,1024]{2,1,0:T(8,128)(2,1)S(1)}, bf16[1,64,1024]{2,1,0:T(8,128)(2,1)S(1)}, u32[]{:S(2)}, u32[]{:S(2)}) collective-permute-start(bf16[1,64,1024]{2,1,0:T(8,128)(2,1)S(1)} %pad_maximum_fusion), channel_id=1, source_target_pairs={{0,1},{1,2},{2,3},{3,4},{4,5},{5,6},{6,7},{7,8},{8,9},{9,10},{10,1... | collective-permute-start | bytes 393224 | tf_op jit(solution)/shard_map/ppermute | solution.py:14
  128.4 6.3 %collective-permute-start.1 = (bf16[1,64,1024]{2,1,0:T(8,128)(2,1)S(1)}, bf16[1,64,1024]{2,1,0:T(8,128)(2,1)S(1)}, u32[]{:S(2)}, u32[]{:S(2)}) collective-permute-start(bf16[1,64,1024]{2,1,0:T(8,128)(2,1)S(1)} %pad_maximum_fusion), channel_id=1, source_target_pairs={{1,0},{2,1},{3,2},{4,3},{5,4},{6,5},{7,6},{8,7},{9,8},{10,9},{11,1... | collective-permute-start | bytes 393224 | tf_op jit(solution)/shard_map/ppermute | solution.py:17
  138.6 6.3 %copy-start.2 = (bf16[256,8]{0,1:T(8,128)(2,1)S(1)}, bf16[256,8]{0,1:T(8,128)(2,1)}, u32[]{:S(2)}) copy-start(bf16[256,8]{0,1:T(8,128)(2,1)} %param.17) | copy-start | bytes 12292
Sparse Core Ops, SparseCore 0:
  64.9 57.5 reduce-scatter.1
where the time goes:
time: 155 us; the launch traced here: 154 us
  blocking collectives  83.5 us (54%)
  waiting for transfers between devices  30.3 us (20%)
  matrix products  15.8 us (10%)
  between operations  14.3 us (9%)
  starting transfers between devices  6.78 us (4%)
  other arithmetic  1.72 us (1%)
    unnamed x1, blocking collectives  30.5 us
    pmax x1, blocking collectives, shards(): largest = lax.pmax(block_peak, 'mem')  29 us
    reduce_scatter x1, waiting for transfers between devices, shards(): lax.psum_scatter(scaled_values, 'mem', scatter_dimension=0, tiled=True)  25.9 us
    all_gather x1, blocking collectives, shards(): lax.all_gather(query_key, 'mem', axis=0, tiled=True).reshape(-1, key_width)  23.9 us
    dot_general x8, matrix products, conv_taps(): jnp.dot(window, weight[row_step, col_step], preferred_element_type=jnp.fl...  10 us
    ppermute x1, starting transfers between devices, with_halo(): lax.ppermute(lax.slice_in_dim(block, block.shape[dim] - width, None, axis...  4.86 us
    ppermute x1, waiting for transfers between devices, with_halo(): lax.ppermute(lax.slice_in_dim(block, 0, width, axis=dim), axis, backward)  4.35 us
    dot_general x1, matrix products, shards(): jnp.dot(weights, mem_value, preferred_element_type=jnp.float32)  3.38 us
  transfers between devices with their start and end apart: 3, of which 2 were waited for; matrix products, arithmetic and copies ran while one was open for 1% of the time, Pallas kernels for 0%

commit v1 on v0

v1 whole, which is shorter than its diff:
```python
import functools
import math

import jax
import jax.numpy as jnp
from jax import lax
from jax.experimental import pallas as pl
from jax.experimental.pallas import tpu as pltpu
from jax.sharding import PartitionSpec as P

F32 = jnp.float32
BF16 = jnp.bfloat16


def bit_xor(a, b, size):
    out, bit = 0, 1
    while bit < size:
        out = out + ((a // bit + b // bit) % 2) * bit
        bit *= 2
    return out


def remote(src, dst, send, recv, target):
    return pltpu.make_async_remote_copy(
        src_ref=src,
        dst_ref=dst,
        send_sem=send,
        recv_sem=recv,
        device_id={"mem": target},
        device_id_type=pl.DeviceIdType.MESH,
    )


def kernel(
    n,
    count_ref,
    keys_hbm,
    base_hbm,
    labels_hbm,
    query_hbm,
    qval_hbm,
    embed_hbm,
    weight_hbm,
    mask_hbm,
    out_ref,
    keys_ref,
    base_ref,
    labels_ref,
    query_ref,
    qval_ref,
    embed_ref,
    weight,
    mask_ref,
    load_sem,
    values,
    sib_keys,
    sib_values,
    bias,
    sib_bias,
    queries,
    send_vals,
    send_stats,
    recv_vals,
    recv_stats,
    halo_q,
    halo_r,
    readout,
    acc,
    sib_send,
    sib_recv,
    query_send,
    query_recv,
    vals_send,
    vals_recv,
    stats_send,
    stats_recv,
    haloq_send,
    haloq_recv,
    halor_send,
    halor_recv,
):
    chips = n // 2
    zs = chips // 2
    me = lax.axis_index("mem")
    core = me % 2
    chip = me // 2
    y = chip % 2
    z = chip // 2
    sibling = me + 1 - 2 * core
    other = me - 1 + 2 * core
    has_other = jnp.logical_and(other >= 0, other < n)
    width, val = qval_ref.shape
    scale = 1.0 / math.sqrt(keys_ref.shape[1])

    barrier = pltpu.get_barrier_semaphore()

    def greet(target):
        pl.semaphore_signal(
            barrier, inc=1, device_id={"mem": target}, device_id_type=pl.DeviceIdType.MESH
        )

    greet(sibling)
    for d in range(1, chips):
        greet(bit_xor(chip, d, chips) * 2 + core)

    @pl.when(has_other)
    def _():
        greet(other)

    loads = [
        pltpu.make_async_copy(src, dst, load_sem.at[k])
        for k, (src, dst) in enumerate(
            (
                (query_hbm, query_ref),
                (labels_hbm, labels_ref),
                (embed_hbm, embed_ref),
                (base_hbm, base_ref),
                (keys_hbm, keys_ref),
                (qval_hbm, qval_ref),
                (mask_hbm, mask_ref),
                (weight_hbm, weight),
            )
        )
    ]
    for load in loads:
        load.start()
    for load in loads[:4]:
        load.wait()

    objects = embed_ref.shape[0]
    embed = embed_ref[...].astype(F32)
    cols = labels_ref.shape[1]
    for row in range(labels_ref.shape[0]):
        lab = jnp.broadcast_to(labels_ref[row : row + 1, :], (objects, cols))
        onehot = (lab == lax.broadcasted_iota(jnp.int32, (objects, cols), 0)).astype(F32)
        added = lax.dot_general(
            onehot, embed, (((0,), (0,)), ((), ())), preferred_element_type=F32
        )
        part = pl.ds(row * cols, cols)
        values[part, :] = (base_ref[part, :].astype(F32) + added).astype(BF16)
    place = lax.broadcasted_iota(jnp.int32, bias.shape, 1)
    bias[...] = jnp.where(place < count_ref[0], 0.0, -jnp.inf).astype(F32)
    queries[chip] = query_ref[...]

    for load in loads[4:6]:
        load.wait()
    pl.semaphore_wait(barrier, chips + has_other.astype(jnp.int32))

    def query_copy(d):
        peer = bit_xor(chip, d, chips)
        send = remote(
            query_ref, queries.at[chip], query_send.at[peer], query_recv.at[chip], peer * 2 + core
        )
        recv = remote(
            query_ref, queries.at[peer], query_send.at[peer], query_recv.at[peer], peer * 2 + core
        )
        return send, recv

    for d in range(chips - 1, 0, -1):
        query_copy(d)[0].start()
    sib_copies = [
        remote(src, dst, sib_send.at[k], sib_recv.at[k], sibling)
        for k, (src, dst) in enumerate(
            ((keys_ref, sib_keys), (bias, sib_bias), (values, sib_values))
        )
    ]
    for copy in sib_copies:
        copy.start()

    def halo_copies(src, buf, send, recv):
        to_sib = remote(src, buf.at[core], send.at[0], recv.at[core], sibling)
        from_sib = remote(src, buf.at[1 - core], send.at[0], recv.at[1 - core], sibling)
        to_other = remote(src, buf.at[1 - core], send.at[1], recv.at[1 - core], other)
        from_other = remote(src, buf.at[core], send.at[1], recv.at[core], other)
        return to_sib, from_sib, to_other, from_other

    q_sib, q_from_sib, q_other, q_from_other = halo_copies(qval_ref, halo_q, haloq_send, haloq_recv)
    q_sib.start()

    @pl.when(has_other)
    def _():
        q_other.start()

    @pl.when(jnp.logical_not(has_other))
    def _():
        halo_q[core] = jnp.zeros((width, val), BF16)
        halo_r[core] = jnp.zeros((width, val), BF16)

    def wait_query(target_chip):
        remote(
            query_ref,
            queries.at[target_chip],
            query_send.at[target_chip],
            query_recv.at[target_chip],
            target_chip * 2 + core,
        ).wait_recv()

    def vals_copies(target):
        return (
            remote(
                send_vals.at[target],
                recv_vals.at[chip],
                vals_send.at[target],
                vals_recv.at[chip],
                target * 2 + core,
            ),
            remote(
                send_stats.at[target // 2],
                recv_stats.at[chip],
                stats_send.at[target],
                stats_recv.at[chip],
                target * 2 + core,
            ),
        )

    def step(k, carry):
        d = zs - 1 - k
        zt = bit_xor(z, d, zs)
        for yt in range(2):

            @pl.when(zt * 2 + yt != chip)
            def _():
                wait_query(zt * 2 + yt)

        @pl.when(k == 0)
        def _():
            for copy in sib_copies:
                copy.wait_recv()

        q = queries[pl.ds(zt * 2, 2)].reshape(2 * width, -1)
        contract = (((1,), (1,)), ((), ()))
        s0 = lax.dot_general(q, keys_ref[...], contract, preferred_element_type=F32)
        s1 = lax.dot_general(q, sib_keys[...], contract, preferred_element_type=F32)
        s0 = s0 * scale + bias[0:1, :]
        s1 = s1 * scale + sib_bias[0:1, :]
        peak = jnp.maximum(
            jnp.max(s0, axis=1, keepdims=True), jnp.max(s1, axis=1, keepdims=True)
        )
        w0 = jnp.exp(s0 - peak).astype(BF16)
        w1 = jnp.exp(s1 - peak).astype(BF16)
        mass = jnp.sum(w0.astype(F32) + w1.astype(F32), axis=1, keepdims=True)
        summed = jnp.dot(w0, values[...], preferred_element_type=F32) + jnp.dot(
            w1, sib_values[...], preferred_element_type=F32
        )
        send_vals[pl.ds(zt * 2, 2)] = summed.astype(BF16).reshape(2, width, val)
        lane = lax.broadcasted_iota(jnp.int32, (2 * width, 128), 1)
        stats = jnp.where(lane == 0, peak, mass)
        send_stats[zt] = stats.T[0:8, :]
        for yt in range(2):
            target = zt * 2 + yt

            @pl.when(target != chip)
            def _():
                for copy in vals_copies(target):
                    copy.start()

        return carry

    lax.fori_loop(0, zs, step, 0)
    recv_vals[chip] = send_vals[chip]
    recv_stats[chip] = send_stats[z]

    for load in loads[6:]:
        load.wait()
    q_from_sib.wait_recv()

    @pl.when(has_other)
    def _():
        q_from_other.wait_recv()

    for dc in range(3):
        total = jnp.zeros((width, acc.shape[2]), F32)
        for dr, src in enumerate((halo_q.at[0], qval_ref, halo_q.at[1])):
            total += jnp.dot(src[...], weight[dr, dc, val:, :], preferred_element_type=F32)
        acc[dc] = total

    for d in range(1, chips):
        peer = bit_xor(chip, d, chips)
        remote(
            send_vals.at[peer], recv_vals.at[peer], vals_send.at[peer], vals_recv.at[peer],
            peer * 2 + core,
        ).wait_recv()
        remote(
            send_stats.at[peer // 2], recv_stats.at[peer], stats_send.at[peer],
            stats_recv.at[peer], peer * 2 + core,
        ).wait_recv()

    peaks, masses = [], []
    for first in range(0, chips, 16):
        tiles = recv_stats[first : min(first + 16, chips)].reshape(-1, 2 * width)
        have = tiles.shape[0] // 8
        tiles = jnp.concatenate([tiles] * (16 // have), axis=0)
        turned = tiles.T
        turned = jnp.where(y == 0, turned[:width], turned[width:])
        for k in range(have):
            peaks.append(turned[:, k * 8 : k * 8 + 1])
            masses.append(turned[:, k * 8 + 1 : k * 8 + 2])
    largest = functools.reduce(jnp.maximum, peaks)
    weight_sum = jnp.zeros((width, 1), F32)
    value_sum = jnp.zeros((width, val), F32)
    for k in range(chips):
        factor = jnp.exp(peaks[k] - largest)
        weight_sum += factor * masses[k]
        value_sum += factor * recv_vals[k].astype(F32)
    readout[...] = (value_sum / weight_sum).astype(BF16)

    r_sib, r_from_sib, r_other, r_from_other = halo_copies(readout, halo_r, halor_send, halor_recv)

    @pl.when(has_other)
    def _():
        r_other.start()

    r_sib.start()
    for dc in range(3):
        acc[dc] += jnp.dot(readout[...], weight[1, dc, :val, :], preferred_element_type=F32)
    r_from_sib.wait_recv()

    @pl.when(has_other)
    def _():
        r_from_other.wait_recv()

    taps = []
    for dc in range(3):
        total = acc[dc]
        for dr, slot in ((0, 0), (2, 1)):
            total += jnp.dot(halo_r[slot], weight[dr, dc, :val, :], preferred_element_type=F32)
        taps.append(total)
    zero = jnp.zeros((1, acc.shape[2]), F32)
    summed = (
        jnp.concatenate([zero, taps[0][:-1]], axis=0)
        + taps[1]
        + jnp.concatenate([taps[2][1:], zero], axis=0)
    )
    hidden = jnp.maximum(summed, 0.0).astype(BF16)
    out_ref[...] = lax.dot_general(
        mask_ref[...], hidden, (((1,), (1,)), ((), ())), preferred_element_type=F32
    )

    for d in range(1, chips):
        query_copy(d)[0].wait_send()
        for copy in vals_copies(bit_xor(chip, d, chips)):
            copy.wait_send()
    for copy in sib_copies:
        copy.wait_send()
    q_sib.wait_send()
    r_sib.wait_send()

    @pl.when(has_other)
    def _():
        q_other.wait_send()
        r_other.wait_send()


def shards(
    mem_key,
    value_base,
    memory_labels,
    valid_counts,
    query_key,
    query_value,
    object_embed,
    decode_weight,
    mask_weight,
):
    n = lax.axis_size("mem")
    chips = n // 2
    key_width = mem_key.shape[2]
    val = value_base.shape[2]
    height, width = query_value.shape[:2]
    keys = mem_key.reshape(-1, key_width)
    base = value_base.reshape(-1, val)
    block = keys.shape[0]
    dec = decode_weight.shape[3]
    hbm = pl.BlockSpec(memory_space=pltpu.HBM)
    queries = query_key.reshape(-1, key_width)
    query_values = query_value.reshape(-1, val)
    mask = mask_weight.T
    staged = (keys, base, memory_labels, queries, query_values, object_embed, decode_weight, mask)
    dma = pltpu.SemaphoreType.DMA
    out = pl.pallas_call(
        functools.partial(kernel, n),
        out_shape=jax.ShapeDtypeStruct((mask_weight.shape[1], height * width), F32),
        in_specs=[pl.BlockSpec(memory_space=pltpu.SMEM)] + [hbm] * len(staged),
        out_specs=pl.BlockSpec(memory_space=pltpu.VMEM),
        scratch_shapes=[pltpu.VMEM(array.shape, array.dtype) for array in staged]
        + [
            dma((len(staged),)),
            pltpu.VMEM((block, val), BF16),
            pltpu.VMEM((block, key_width), BF16),
            pltpu.VMEM((block, val), BF16),
            pltpu.VMEM((8, block), F32),
            pltpu.VMEM((8, block), F32),
            pltpu.VMEM((chips, width, key_width), BF16),
            pltpu.VMEM((chips, width, val), BF16),
            pltpu.VMEM((chips // 2, 8, 2 * width), F32),
            pltpu.VMEM((chips, width, val), BF16),
            pltpu.VMEM((chips, 8, 2 * width), F32),
            pltpu.VMEM((2, width, val), BF16),
            pltpu.VMEM((2, width, val), BF16),
            pltpu.VMEM((width, val), BF16),
            pltpu.VMEM((3, width, dec), F32),
            dma((3,)),
            dma((3,)),
            dma((chips,)),
            dma((chips,)),
            dma((chips,)),
            dma((chips,)),
            dma((chips,)),
            dma((chips,)),
            dma((2,)),
            dma((2,)),
            dma((2,)),
            dma((2,)),
        ],
        compiler_params=pltpu.CompilerParams(
            collective_id=0, has_side_effects=True, vmem_limit_bytes=48 * 1024 * 1024
        ),
    )(valid_counts, *staged)
    return out.T.reshape(height, width, mask_weight.shape[1])


def solution(mesh):
    rows = ("groups", "mem")
    placed = (
        P(rows, None, None),
        P(rows, None, None),
        P(rows, None),
        P(rows),
        P(rows, None, None),
        P(rows, None, None),
        P(),
        P(),
        P(),
    )
    return jax.shard_map(
        shards,
        mesh=mesh,
        in_specs=placed,
        out_specs=P(rows, None, None),
        check_vma=False,
    )
```

time: 155 us -> 36.9 us (0.24)
  blocking collectives: 83.5 us -> 0 us
  waiting for transfers between devices: 30.3 us -> 0 us
  Pallas kernels: 0 us -> 27.3 us
  matrix products: 15.8 us -> 0 us
  between operations: 14.3 us -> 0.68 us
  local copies, waits for them, and re-layouts: 1.34 us -> 8.49 us
  starting transfers between devices: 6.78 us -> 0 us
  other arithmetic: 1.72 us -> 0 us
    unnamed x1 -> x0, blocking collectives: 30.5 us -> none
    pmax x1 -> x0, blocking collectives: 29 us -> none  [shards(): largest = lax.pmax(block_peak, 'mem')]
    pallas_call x0 -> x1, Pallas kernels: none -> 27.3 us  [shards(): pl.pallas_call(functools.partial(kernel, n), out_shape=jax.ShapeDtypeStru...]
    reduce_scatter x1 -> x0, waiting for transfers between devices: 25.9 us -> none  [shards(): lax.psum_scatter(scaled_values, 'mem', scatter_dimension=0, tiled=True)]
    all_gather x1 -> x0, blocking collectives: 23.9 us -> none  [shards(): lax.all_gather(query_key, 'mem', axis=0, tiled=True).reshape(-1, key_width)]
    dot_general x11 -> x0, matrix products: 15.8 us -> none  [the longest x8 10 us: conv_taps(): jnp.dot(window, weight[row_step, col_step], preferred_element_type=jnp.fl...]
    unnamed x13 -> x17, local copies, waits for them, and re-layouts: 0.62 us -> 8.49 us
    ppermute x2 -> x0, starting transfers between devices: 6.78 us -> none  [the longest x1 4.86 us: with_halo(): lax.ppermute(lax.slice_in_dim(block, block.shape[dim] - width, None, axis...]
  transfers between devices with their start and end apart: 3 -> 0, of which waited for: 2 -> 0; matrix products, arithmetic and copies ran while one was open for 1% -> 0% of each run, Pallas kernels for 0% -> 0%
where the time goes in v1:
time: 36.9 us; the launch traced here: 36.4 us
  Pallas kernels  27.3 us (74%)
  local copies, waits for them, and re-layouts  8.49 us (23%)
  between operations  0.68 us (2%)
    pallas_call x1, Pallas kernels, shards(): pl.pallas_call(functools.partial(kernel, n), out_shape=jax.ShapeDtypeStru...  27.3 us
    unnamed x17, local copies, waits for them, and re-layouts  8.49 us

profile of v1, /device:TPU:1, one launch (start us, length us, event | category | flops | bytes accessed | tf_op | source)
XLA Modules:
  0.0 36.4 jit_solution(14691568439529401874)
XLA Ops:
  0.7 0.0 copy-start
  0.7 2.3 %copy-done = bf16[3,3,1024,256]{3,2,1,0:T(8,128)(2,1)S(1)} copy-done((bf16[3,3,1024,256]{3,2,1,0:T(8,128)(2,1)S(1)}, bf16[3,3,1024,256]{3,2,1,0:T(8,128)(2,1)}, u32[]{:S(2)}) %copy-start) | copy-done | bytes 4718616
  3.0 0.0 copy-start.1
  3.0 1.0 %copy-done.1 = bf16[4,128,512]{2,1,0:T(8,128)(2,1)S(1)} copy-done((bf16[4,128,512]{2,1,0:T(8,128)(2,1)S(1)}, bf16[4,128,512]{2,1,0:T(8,128)(2,1)}, u32[]{:S(2)}) %copy-start.1) | copy-done | bytes 524312
  4.0 0.0 copy-start.2
  4.0 0.9 %copy-done.2 = bf16[4,128,128]{2,1,0:T(8,128)(2,1)S(1)} copy-done((bf16[4,128,128]{2,1,0:T(8,128)(2,1)S(1)}, bf16[4,128,128]{2,1,0:T(8,128)(2,1)}, u32[]{:S(2)}) %copy-start.2) | copy-done | bytes 131096
  4.9 0.0 copy-start.3
  4.9 0.8 %copy-done.3 = bf16[1,64,512]{2,1,0:T(8,128)(2,1)S(1)} copy-done((bf16[1,64,512]{2,1,0:T(8,128)(2,1)S(1)}, bf16[1,64,512]{2,1,0:T(8,128)(2,1)}, u32[]{:S(2)}) %copy-start.3) | copy-done | bytes 65560
  5.8 0.0 copy-start.4
  5.8 0.7 %copy-done.4 = bf16[1,64,128]{2,1,0:T(8,128)(2,1)S(1)} copy-done((bf16[1,64,128]{2,1,0:T(8,128)(2,1)S(1)}, bf16[1,64,128]{2,1,0:T(8,128)(2,1)}, u32[]{:S(2)}) %copy-start.4) | copy-done | bytes 16408
  6.5 0.0 copy-start.5
  6.5 0.7 %copy-done.5 = bf16[8,512]{1,0:T(8,128)(2,1)S(1)} copy-done((bf16[8,512]{1,0:T(8,128)(2,1)S(1)}, bf16[8,512]{1,0:T(8,128)(2,1)}, u32[]{:S(2)}) %copy-start.5) | copy-done | bytes 8216
  7.2 0.0 copy-start.6
  7.2 0.7 %copy-done.6 = bf16[256,8]{0,1:T(8,128)(2,1)S(1)} copy-done((bf16[256,8]{0,1:T(8,128)(2,1)S(1)}, bf16[256,8]{0,1:T(8,128)(2,1)}, u32[]{:S(2)}) %copy-start.6) | copy-done | bytes 4120
  7.9 0.0 copy-start.7
  7.9 0.7 %copy-done.7 = s32[4,128]{1,0:T(4,128)S(1)} copy-done((s32[4,128]{1,0:T(4,128)S(1)}, s32[4,128]{1,0:T(4,128)}, u32[]{:S(2)}) %copy-start.7) | copy-done | bytes 2072
  8.6 27.3 %shard_map.91 = f32[8,64]{1,0:T(8,128)S(1)} custom-call(s32[1]{0:T(128)S(6)} %copy.11.count_ref, bf16[512,128]{1,0:T(8,128)(2,1)S(1)} %bitcast.9, bf16[512,512]{1,0:T(8,128)(2,1)S(1)} %bitcast.8, s32[4,128]{1,0:T(4,128)S(1)} %copy-done.7, bf16[64,128]{1,0:T(8,128)(2,1)S(1)} %bitcast.11, bf16[64,512]{1,0:T(8,128)(2,1)S(1)} %bitcast.10, ...), custom_call_target="tpu_custom_call" | custom-call | tf_op jit(solution)/shard_map/pallas_call | solution.py:380
  35.8 0.6 %copy.12 = f32[1,64,8]{1,2,0:T(8,128)} copy(f32[1,64,8]{1,2,0:T(8,128)S(1)} %bitcast.12) | data formatting | bytes 4096
Async XLA Ops:
  0.7 2.3 %copy-start = (bf16[3,3,1024,256]{3,2,1,0:T(8,128)(2,1)S(1)}, bf16[3,3,1024,256]{3,2,1,0:T(8,128)(2,1)}, u32[]{:S(2)}) copy-start(bf16[3,3,1024,256]{3,2,1,0:T(8,128)(2,1)} %weight_hbm.1) | copy-start | bytes 14155780
  3.0 1.0 %copy-start.1 = (bf16[4,128,512]{2,1,0:T(8,128)(2,1)S(1)}, bf16[4,128,512]{2,1,0:T(8,128)(2,1)}, u32[]{:S(2)}) copy-start(bf16[4,128,512]{2,1,0:T(8,128)(2,1)} %param.10) | copy-start | bytes 1572868
  4.0 0.9 %copy-start.2 = (bf16[4,128,128]{2,1,0:T(8,128)(2,1)S(1)}, bf16[4,128,128]{2,1,0:T(8,128)(2,1)}, u32[]{:S(2)}) copy-start(bf16[4,128,128]{2,1,0:T(8,128)(2,1)} %param.9) | copy-start | bytes 393220
  4.9 0.8 %copy-start.3 = (bf16[1,64,512]{2,1,0:T(8,128)(2,1)S(1)}, bf16[1,64,512]{2,1,0:T(8,128)(2,1)}, u32[]{:S(2)}) copy-start(bf16[1,64,512]{2,1,0:T(8,128)(2,1)} %param.14) | copy-start | bytes 196612
  5.8 0.7 %copy-start.4 = (bf16[1,64,128]{2,1,0:T(8,128)(2,1)S(1)}, bf16[1,64,128]{2,1,0:T(8,128)(2,1)}, u32[]{:S(2)}) copy-start(bf16[1,64,128]{2,1,0:T(8,128)(2,1)} %param.13) | copy-start | bytes 49156
  6.5 0.7 %copy-start.5 = (bf16[8,512]{1,0:T(8,128)(2,1)S(1)}, bf16[8,512]{1,0:T(8,128)(2,1)}, u32[]{:S(2)}) copy-start(bf16[8,512]{1,0:T(8,128)(2,1)} %embed_hbm.1) | copy-start | bytes 24580
  7.2 0.7 %copy-start.6 = (bf16[256,8]{0,1:T(8,128)(2,1)S(1)}, bf16[256,8]{0,1:T(8,128)(2,1)}, u32[]{:S(2)}) copy-start(bf16[256,8]{0,1:T(8,128)(2,1)} %param.17) | copy-start | bytes 12292
  7.9 0.7 %copy-start.7 = (s32[4,128]{1,0:T(4,128)S(1)}, s32[4,128]{1,0:T(4,128)}, u32[]{:S(2)}) copy-start(s32[4,128]{1,0:T(4,128)} %labels_hbm.1) | copy-start | bytes 6148

commit v2 on v1

--- a/solution.py
+++ b/solution.py
@@ -413,7 +413,7 @@
             dma((2,)),
         ],
         compiler_params=pltpu.CompilerParams(
-            collective_id=0, has_side_effects=True, vmem_limit_bytes=48 * 1024 * 1024
+            collective_id=0, has_side_effects=True, vmem_limit_bytes=60 * 1024 * 1024
         ),
     )(valid_counts, *staged)
     return out.T.reshape(height, width, mask_weight.shape[1])

time: 36.9 us -> 30.2 us (0.82)
  local copies, waits for them, and re-layouts: 8.49 us -> 1.28 us
  Pallas kernels: 27.3 us -> 28 us
    unnamed x17 -> x1, local copies, waits for them, and re-layouts: 8.49 us -> 1.28 us
    pallas_call x1, Pallas kernels: 27.3 us -> 28 us  [shards(): pl.pallas_call(functools.partial(kernel, n), out_shape=jax.ShapeDtypeStru...]
where the time goes in v2:
time: 30.2 us; the launch traced here: 29.9 us
  Pallas kernels  28 us (93%)
  local copies, waits for them, and re-layouts  1.28 us (4%)
  between operations  0.66 us (2%)
    pallas_call x1, Pallas kernels, shards(): pl.pallas_call(functools.partial(kernel, n), out_shape=jax.ShapeDtypeStru...  28 us
    unnamed x1, local copies, waits for them, and re-layouts  1.28 us

profile of v2, /device:TPU:1, one launch (start us, length us, event | category | flops | bytes accessed | tf_op | source)
XLA Modules:
  0.0 29.9 jit_solution(8327158700943516417)
XLA Ops:
  0.7 28.0 %shard_map.91 = f32[8,64]{1,0:T(8,128)} custom-call(s32[1]{0:T(128)S(6)} %copy.11.count_ref, bf16[512,128]{1,0:T(8,128)(2,1)} %bitcast.9, bf16[512,512]{1,0:T(8,128)(2,1)} %bitcast.8, s32[4,128]{1,0:T(4,128)} %labels_hbm.1, bf16[64,128]{1,0:T(8,128)(2,1)} %bitcast.11, bf16[64,512]{1,0:T(8,128)(2,1)} %bitcast.10, bf16[8,512]{1,0:T(8,128)(2,1)} %embed_hbm.1, ...), custom_call_target="tpu_custom_call" | custom-call | tf_op jit(solution)/shard_map/pallas_call | solution.py:380
  28.7 1.3 %copy.12 = f32[1,64,8]{1,2,0:T(8,128)} copy(f32[1,64,8]{1,2,0:T(8,128)} %bitcast.12) | data formatting | bytes 4096

commit v3 on v2

--- a/solution.py
+++ b/solution.py
@@ -58,6 +58,11 @@
     bias,
     sib_bias,
     queries,
+    own_vals,
+    own_stats,
+    send_y,
+    recv_y,
+    y_stats,
     send_vals,
     send_stats,
     recv_vals,
@@ -70,6 +75,10 @@
     sib_recv,
     query_send,
     query_recv,
+    y_send,
+    y_recv,
+    ys_send,
+    ys_recv,
     vals_send,
     vals_recv,
     stats_send,
@@ -195,27 +204,39 @@
             target_chip * 2 + core,
         ).wait_recv()
 
-    def vals_copies(target):
+    y_peer = chip + 1 - 2 * y
+
+    def y_copies(zt):
         return (
             remote(
-                send_vals.at[target],
-                recv_vals.at[chip],
-                vals_send.at[target],
-                vals_recv.at[chip],
-                target * 2 + core,
+                send_y.at[zt], recv_y.at[zt], y_send.at[zt], y_recv.at[zt], y_peer * 2 + core
             ),
             remote(
-                send_stats.at[target // 2],
-                recv_stats.at[chip],
-                stats_send.at[target],
-                stats_recv.at[chip],
-                target * 2 + core,
+                own_stats.at[zt],
+                y_stats.at[zt],
+                ys_send.at[zt],
+                ys_recv.at[zt],
+                y_peer * 2 + core,
             ),
         )
 
-    def step(k, carry):
-        d = zs - 1 - k
-        zt = bit_xor(z, d, zs)
+    def z_copies(zt, slot):
+        target = (zt * 2 + y) * 2 + core
+        return (
+            remote(
+                send_vals.at[zt], recv_vals.at[slot], vals_send.at[zt], vals_recv.at[slot], target
+            ),
+            remote(
+                send_stats.at[zt],
+                recv_stats.at[slot],
+                stats_send.at[zt],
+                stats_recv.at[slot],
+                target,
+            ),
+        )
+
+    def attend(k, carry):
+        zt = bit_xor(z, zs - 1 - k, zs)
         for yt in range(2):
 
             @pl.when(zt * 2 + yt != chip)
@@ -242,23 +263,50 @@
         summed = jnp.dot(w0, values[...], preferred_element_type=F32) + jnp.dot(
             w1, sib_values[...], preferred_element_type=F32
         )
-        send_vals[pl.ds(zt * 2, 2)] = summed.astype(BF16).reshape(2, width, val)
+        own_vals[zt] = jnp.where(y == 0, summed[:width], summed[width:])
+        send_y[zt] = jnp.where(y == 0, summed[width:], summed[:width]).astype(BF16)
         lane = lax.broadcasted_iota(jnp.int32, (2 * width, 128), 1)
         stats = jnp.where(lane == 0, peak, mass)
-        send_stats[zt] = stats.T[0:8, :]
-        for yt in range(2):
-            target = zt * 2 + yt
-
-            @pl.when(target != chip)
-            def _():
-                for copy in vals_copies(target):
-                    copy.start()
-
+        own_stats[zt] = stats.T[0:8, :]
+        for copy in y_copies(zt):
+            copy.start()
         return carry
 
-    lax.fori_loop(0, zs, step, 0)
-    recv_vals[chip] = send_vals[chip]
-    recv_stats[chip] = send_stats[z]
+    lax.fori_loop(0, zs, attend, 0)
+
+    def merge(k, carry):
+        zt = bit_xor(z, zs - 1 - k, zs)
+        for copy in y_copies(zt):
+            copy.wait_recv()
+        mine, theirs = own_stats[zt], y_stats[zt]
+        turned = jnp.concatenate([mine, theirs] * (width // 8), axis=0).T
+        turned = jnp.where(y == 0, turned[:width], turned[width:])
+        mine_peak, theirs_peak = turned[:, 0:1], turned[:, 8:9]
+        peak = jnp.maximum(mine_peak, theirs_peak)
+        merged = (
+            jnp.exp(mine_peak - peak) * own_vals[zt]
+            + jnp.exp(theirs_peak - peak) * recv_y[zt].astype(F32)
+        ).astype(BF16)
+        top = jnp.maximum(mine[0:1], theirs[0:1])
+        mass = jnp.exp(mine[0:1] - top) * mine[1:2] + jnp.exp(theirs[0:1] - top) * theirs[1:2]
+        sub = lax.broadcasted_iota(jnp.int32, mine.shape, 0)
+        stats = jnp.where(sub == 0, top, mass)
+
+        @pl.when(zt != z)
+        def _():
+            send_vals[zt] = merged
+            send_stats[zt] = stats
+            for copy in z_copies(zt, z):
+                copy.start()
+
+        @pl.when(zt == z)
+        def _():
+            recv_vals[z] = merged
+            recv_stats[z] = stats
+
+        return carry
+
+    lax.fori_loop(0, zs, merge, 0)
 
     for load in loads[6:]:
         load.wait()
@@ -274,20 +322,14 @@
             total += jnp.dot(src[...], weight[dr, dc, val:, :], preferred_element_type=F32)
         acc[dc] = total
 
-    for d in range(1, chips):
-        peer = bit_xor(chip, d, chips)
-        remote(
-            send_vals.at[peer], recv_vals.at[peer], vals_send.at[peer], vals_recv.at[peer],
-            peer * 2 + core,
-        ).wait_recv()
-        remote(
-            send_stats.at[peer // 2], recv_stats.at[peer], stats_send.at[peer],
-            stats_recv.at[peer], peer * 2 + core,
-        ).wait_recv()
+    for d in range(1, zs):
+        peer = bit_xor(z, d, zs)
+        for copy in z_copies(peer, peer):
+            copy.wait_recv()
 
     peaks, masses = [], []
-    for first in range(0, chips, 16):
-        tiles = recv_stats[first : min(first + 16, chips)].reshape(-1, 2 * width)
+    for first in range(0, zs, 16):
+        tiles = recv_stats[first : min(first + 16, zs)].reshape(-1, 2 * width)
         have = tiles.shape[0] // 8
         tiles = jnp.concatenate([tiles] * (16 // have), axis=0)
         turned = tiles.T
@@ -298,7 +340,7 @@
     largest = functools.reduce(jnp.maximum, peaks)
     weight_sum = jnp.zeros((width, 1), F32)
     value_sum = jnp.zeros((width, val), F32)
-    for k in range(chips):
+    for k in range(zs):
         factor = jnp.exp(peaks[k] - largest)
         weight_sum += factor * masses[k]
         value_sum += factor * recv_vals[k].astype(F32)
@@ -338,7 +380,9 @@
 
     for d in range(1, chips):
         query_copy(d)[0].wait_send()
-        for copy in vals_copies(bit_xor(chip, d, chips)):
+    for d in range(zs):
+        peer = bit_xor(z, d, zs)
+        for copy in y_copies(peer) + (z_copies(peer, z) if d else ()):
             copy.wait_send()
     for copy in sib_copies:
         copy.wait_send()
@@ -364,6 +408,7 @@
 ):
     n = lax.axis_size("mem")
     chips = n // 2
+    zs = chips // 2
     key_width = mem_key.shape[2]
     val = value_base.shape[2]
     height, width = query_value.shape[:2]
@@ -391,10 +436,15 @@
             pltpu.VMEM((8, block), F32),
             pltpu.VMEM((8, block), F32),
             pltpu.VMEM((chips, width, key_width), BF16),
-            pltpu.VMEM((chips, width, val), BF16),
-            pltpu.VMEM((chips // 2, 8, 2 * width), F32),
-            pltpu.VMEM((chips, width, val), BF16),
-            pltpu.VMEM((chips, 8, 2 * width), F32),
+            pltpu.VMEM((zs, width, val), F32),
+            pltpu.VMEM((zs, 8, 2 * width), F32),
+            pltpu.VMEM((zs, width, val), BF16),
+            pltpu.VMEM((zs, width, val), BF16),
+            pltpu.VMEM((zs, 8, 2 * width), F32),
+            pltpu.VMEM((zs, width, val), BF16),
+            pltpu.VMEM((zs, 8, 2 * width), F32),
+            pltpu.VMEM((zs, width, val), BF16),
+            pltpu.VMEM((zs, 8, 2 * width), F32),
             pltpu.VMEM((2, width, val), BF16),
             pltpu.VMEM((2, width, val), BF16),
             pltpu.VMEM((width, val), BF16),
@@ -403,10 +453,14 @@
             dma((3,)),
             dma((chips,)),
             dma((chips,)),
-            dma((chips,)),
-            dma((chips,)),
-            dma((chips,)),
-            dma((chips,)),
+            dma((zs,)),
+            dma((zs,)),
+            dma((zs,)),
+            dma((zs,)),
+            dma((zs,)),
+            dma((zs,)),
+            dma((zs,)),
+            dma((zs,)),
             dma((2,)),
             dma((2,)),
             dma((2,)),

time: 30.2 us -> 27.7 us (0.917)
  Pallas kernels: 28 us -> 25.5 us
    pallas_call x1, Pallas kernels: 28 us -> 25.5 us  [shards(): pl.pallas_call(functools.partial(kernel, n), out_shape=jax.ShapeDtypeStru...]
where the time goes in v3:
time: 27.7 us; the launch traced here: 27.5 us
  Pallas kernels  25.5 us (92%)
  local copies, waits for them, and re-layouts  1.28 us (5%)
  between operations  0.66 us (2%)
    pallas_call x1, Pallas kernels, shards(): pl.pallas_call(functools.partial(kernel, n), out_shape=jax.ShapeDtypeStru...  25.5 us
    unnamed x1, local copies, waits for them, and re-layouts  1.28 us

profile of v3, /device:TPU:1, one launch (start us, length us, event | category | flops | bytes accessed | tf_op | source)
XLA Modules:
  0.0 27.5 jit_solution(5950689736299797584)
XLA Ops:
  0.7 25.5 %shard_map.91 = f32[8,64]{1,0:T(8,128)} custom-call(s32[1]{0:T(128)S(6)} %copy.11.count_ref, bf16[512,128]{1,0:T(8,128)(2,1)} %bitcast.9, bf16[512,512]{1,0:T(8,128)(2,1)} %bitcast.8, s32[4,128]{1,0:T(4,128)} %labels_hbm.1, bf16[64,128]{1,0:T(8,128)(2,1)} %bitcast.11, bf16[64,512]{1,0:T(8,128)(2,1)} %bitcast.10, bf16[8,512]{1,0:T(8,128)(2,1)} %embed_hbm.1, ...), custom_call_target="tpu_custom_call" | custom-call | tf_op jit(solution)/shard_map/pallas_call | solution.py:425
  26.2 1.3 %copy.12 = f32[1,64,8]{1,2,0:T(8,128)} copy(f32[1,64,8]{1,2,0:T(8,128)} %bitcast.12) | data formatting | bytes 4096
